TPU v7x, 256 devices: a whole 4x4x8 slice. The times are simulated.
256 devices in a mesh: shape: 4 (over y), space: 64 (over x, z, core).
Axes of the slice: x: 4, y: 4, z: 8, core: 2. Of those that a mesh axis runs over, the one named last changes fastest.
Arguments:
- features: bfloat16 [4, 128, 512, 128], P('shape', 'space'), may hold values from -45 to 45
- gain_one: float32 [128], replicated, may hold values from 0.1 to 1.9
- weight_one: bfloat16 [7, 128, 128], replicated, may hold values from -0.1875 to 0.1875
- gain_two: float32 [128], replicated, may hold values from 0.1 to 1.9
- weight_two: bfloat16 [7, 128, 128], replicated, may hold values from -0.1875 to 0.1875
- live: int32 [4, 128], P('shape', 'space'), may hold values from 0 to 1, as said below
- send_index: int32 [4, 64, 64, 1], P('shape', 'space'), may hold values from -1 to 11, as said below
- recv_index: int32 [4, 128, 6], P('shape', 'space'), may hold values from -1 to 63, as said below
- cotangent: bfloat16 [4, 128, 512, 128], P('shape', 'space'), may hold values from -6 to 6
Outputs:
- output: bfloat16 [4, 128, 512, 128], P('shape', 'space')
- grad_features: bfloat16 [4, 128, 512, 128], P('shape', 'space')
- grad_weight_one: float32 [7, 128, 128], replicated
- grad_weight_two: float32 [7, 128, 128], replicated
- grad_gain_one: float32 [128], replicated
- grad_gain_two: float32 [128], replicated
Inputs may be any that keep to these rules, and one draw needn't show every extreme that they name: The live slots of each device are its first ones, at least 1 of them; in every shape one device has both slots live and another only 1. `recv_index`: -1 where the face has no neighbour slab, always so on slots that are not live; else a position r of the device's receive buffer of 64 slabs, r being the sending device (one slab per sender). No two faces of one device share a position; on every device the slot from some sender is in use; slot 0 of every device has all six faces. send_index[s, d, e, c] is -1 where slot c from device d to device e is unused, else 6 b + f for a live slot b of device d, f being the opposite of the face of the brick of e that reads that slot; it agrees with recv_index.
All inputs are finite; a program needn't handle non-finite values.
Results may differ from a plain program's by a relative error of at most 0.014.
Values may be sent and summed in bfloat16 or wider, within the bound.
A program may use at most 64 MiB of HBM per device.

v0:
```python
import math
import jax
import jax.numpy as jnp
from jax import lax
from jax.sharding import PartitionSpec as P

EDGE = 8
OFFSETS = ((0, 0, 0), (-1, 0, 0), (1, 0, 0), (0, -1, 0), (0, 1, 0), (0, 0, -1), (0, 0, 1))
norm_epsilon = 1e-05


def pre_act(values, gain):
    row_mean = jnp.mean(values, axis=-1, keepdims=True)
    centered = values - row_mean
    variance = jnp.mean(centered * centered, axis=-1, keepdims=True)
    return jax.nn.silu(centered * lax.rsqrt(variance + norm_epsilon) * gain)


def pre_back(brick_cube, gain, upstream):
    outputs, pullback = jax.vjp(pre_act, brick_cube.astype(jnp.float32), gain)
    return pullback(upstream)


def face_slabs(brick_cube):
    brick_count = brick_cube.shape[0]
    edge_len = brick_cube.shape[1]
    last_layer = edge_len - 1
    face_list = [
        brick_cube[:, 0],
        brick_cube[:, last_layer],
        brick_cube[:, :, 0],
        brick_cube[:, :, last_layer],
        brick_cube[:, :, :, 0],
        brick_cube[:, :, :, last_layer],
    ]
    return jnp.stack(
        [
            face_part.reshape(brick_count, edge_len * edge_len, brick_cube.shape[-1])
            for face_part in face_list
        ],
        axis=1,
    )


def pad_cube(brick_cube, halo_slabs):
    brick_count = brick_cube.shape[0]
    edge_len = brick_cube.shape[1]
    channels = brick_cube.shape[-1]
    slab_grid = halo_slabs.reshape(brick_count, 6, edge_len, edge_len, channels)
    far_side = edge_len + 1
    inside = slice(1, far_side)
    padded = jnp.pad(brick_cube, ((0, 0), (1, 1), (1, 1), (1, 1), (0, 0)))
    padded = padded.at[:, 0, inside, inside].set(slab_grid[:, 0])
    padded = padded.at[:, far_side, inside, inside].set(slab_grid[:, 1])
    padded = padded.at[:, inside, 0, inside].set(slab_grid[:, 2])
    padded = padded.at[:, inside, far_side, inside].set(slab_grid[:, 3])
    padded = padded.at[:, inside, inside, 0].set(slab_grid[:, 4])
    padded = padded.at[:, inside, inside, far_side].set(slab_grid[:, 5])
    return padded


def add_faces(volume, face_terms):
    brick_count = volume.shape[0]
    edge_len = volume.shape[1]
    channels = volume.shape[-1]
    term_grid = face_terms.reshape(brick_count, 6, edge_len, edge_len, channels)
    last_layer = edge_len - 1
    volume = volume.at[:, 0].add(term_grid[:, 0])
    volume = volume.at[:, last_layer].add(term_grid[:, 1])
    volume = volume.at[:, :, 0].add(term_grid[:, 2])
    volume = volume.at[:, :, last_layer].add(term_grid[:, 3])
    volume = volume.at[:, :, :, 0].add(term_grid[:, 4])
    volume = volume.at[:, :, :, last_layer].add(term_grid[:, 5])
    return volume


def shifted(padded, tap_index):
    step_i, step_j, step_k = OFFSETS[tap_index]
    edge_len = padded.shape[1] - 2
    window = padded[
        :,
        1 + step_i : 1 + step_i + edge_len,
        1 + step_j : 1 + step_j + edge_len,
        1 + step_k : 1 + step_k + edge_len,
    ]
    return window.reshape(-1, padded.shape[-1])


def convolve(padded, weight):
    running = jnp.dot(shifted(padded, 0), weight[0], preferred_element_type=jnp.float32)
    for tap_index in range(1, len(OFFSETS)):
        running = running + jnp.dot(
            shifted(padded, tap_index), weight[tap_index], preferred_element_type=jnp.float32
        )
    return running


def conv_back(padded, grad_rows, weight):
    brick_count = padded.shape[0]
    edge_len = padded.shape[1] - 2
    channels = padded.shape[-1]
    weight_grad = jnp.stack(
        [
            lax.dot_general(
                shifted(padded, tap_index),
                grad_rows,
                (((0,), (0,)), ((), ())),
                preferred_element_type=jnp.float32,
            )
            for tap_index in range(len(OFFSETS))
        ]
    )
    spread = jnp.zeros(padded.shape, jnp.float32)
    for tap_index in range(len(OFFSETS)):
        step_i, step_j, step_k = OFFSETS[tap_index]
        tap_term = lax.dot_general(
            grad_rows,
            weight[tap_index],
            (((1,), (1,)), ((), ())),
            preferred_element_type=jnp.float32,
        )
        tap_term = tap_term.reshape(brick_count, edge_len, edge_len, edge_len, channels)
        spread = spread.at[
            :,
            1 + step_i : 1 + step_i + edge_len,
            1 + step_j : 1 + step_j + edge_len,
            1 + step_k : 1 + step_k + edge_len,
        ].add(tap_term)
    far_side = edge_len + 1
    inside = slice(1, far_side)
    interior = spread[:, inside, inside, inside]
    face_list = [
        spread[:, 0, inside, inside],
        spread[:, far_side, inside, inside],
        spread[:, inside, 0, inside],
        spread[:, inside, far_side, inside],
        spread[:, inside, inside, 0],
        spread[:, inside, inside, far_side],
    ]
    halo_grad = jnp.stack(
        [face_part.reshape(brick_count, edge_len * edge_len, channels) for face_part in face_list],
        axis=1,
    ).astype(jnp.bfloat16)
    return (weight_grad, interior, halo_grad)


def trade_faces(brick_cube, send_pick, recv_pick, peer_count, slot_count):
    face_rows = face_slabs(brick_cube)
    flat_rows = face_rows.reshape(send_pick.shape[1], -1)
    outgoing = jnp.dot(send_pick, flat_rows, preferred_element_type=jnp.float32).astype(
        jnp.bfloat16
    )
    incoming = lax.all_to_all(
        outgoing.reshape(peer_count, slot_count, -1),
        "space",
        split_axis=0,
        concat_axis=0,
        tiled=True,
    )
    halo_slabs = jnp.dot(
        recv_pick, incoming.reshape(peer_count * slot_count, -1), preferred_element_type=jnp.float32
    ).astype(jnp.bfloat16)
    return halo_slabs.reshape(face_rows.shape)


def return_slabs(halo_grad, send_pick, recv_pick, peer_count, slot_count):
    flat_rows = halo_grad.reshape(recv_pick.shape[0], -1)
    outgoing = lax.dot_general(
        recv_pick, flat_rows, (((0,), (0,)), ((), ())), preferred_element_type=jnp.float32
    ).astype(jnp.bfloat16)
    incoming = lax.all_to_all(
        outgoing.reshape(peer_count, slot_count, -1),
        "space",
        split_axis=0,
        concat_axis=0,
        tiled=True,
    )
    summed = lax.dot_general(
        send_pick,
        incoming.reshape(peer_count * slot_count, -1),
        (((0,), (0,)), ((), ())),
        preferred_element_type=jnp.float32,
    )
    return summed.reshape(halo_grad.shape)


def forward_conv(brick_cube, weight, send_pick, recv_pick, peer_count, slot_count):
    halo_slabs = trade_faces(brick_cube, send_pick, recv_pick, peer_count, slot_count)
    padded = pad_cube(brick_cube, halo_slabs)
    result = convolve(padded, weight).reshape(brick_cube.shape)
    return (result, padded)


def shards(
    features, gain_one, weight_one, gain_two, weight_two, live, send_index, recv_index, cotangent
):
    brick_count = features.shape[1]
    channels = features.shape[3]
    edge_len = EDGE
    peer_count = lax.axis_size("space")
    slot_count = send_index.shape[3]
    cube_shape = (brick_count, edge_len, edge_len, edge_len, channels)
    cubes_in = features.reshape(cube_shape)
    cot_cube = cotangent.reshape(cube_shape)
    alive_rows = (live.reshape(brick_count) > 0)[:, None, None, None, None]
    send_codes = send_index.reshape(peer_count * slot_count)
    places = recv_index.reshape(brick_count * 6)
    send_pick = (
        send_codes[:, None] == jnp.arange(brick_count * 6, dtype=jnp.int32)[None, :]
    ).astype(jnp.bfloat16)
    recv_pick = (
        places[:, None] == jnp.arange(peer_count * slot_count, dtype=jnp.int32)[None, :]
    ).astype(jnp.bfloat16)
    acts_one = pre_act(cubes_in.astype(jnp.float32), gain_one).astype(jnp.bfloat16)
    conv_one, padded_one = forward_conv(
        acts_one, weight_one, send_pick, recv_pick, peer_count, slot_count
    )
    hidden = conv_one.astype(jnp.bfloat16)
    acts_two = pre_act(hidden.astype(jnp.float32), gain_two).astype(jnp.bfloat16)
    conv_two, padded_two = forward_conv(
        acts_two, weight_two, send_pick, recv_pick, peer_count, slot_count
    )
    output = jnp.where(
        alive_rows, cubes_in.astype(jnp.float32) + conv_two, jnp.zeros(conv_two.shape, jnp.float32)
    ).astype(jnp.bfloat16)
    grad_rows = jnp.where(alive_rows, cot_cube, jnp.zeros_like(cot_cube))
    weight_grad_two, interior_two, halo_grad_two = conv_back(
        padded_two, grad_rows.reshape(-1, channels), weight_two
    )
    returned_two = return_slabs(halo_grad_two, send_pick, recv_pick, peer_count, slot_count)
    grad_hidden, gain_grad_two = pre_back(hidden, gain_two, add_faces(interior_two, returned_two))
    grad_hidden = grad_hidden.astype(jnp.bfloat16)
    weight_grad_one, interior_one, halo_grad_one = conv_back(
        padded_one, grad_hidden.reshape(-1, channels), weight_one
    )
    returned_one = return_slabs(halo_grad_one, send_pick, recv_pick, peer_count, slot_count)
    grad_input, gain_grad_one = pre_back(cubes_in, gain_one, add_faces(interior_one, returned_one))
    direct = jnp.where(
        alive_rows, cot_cube.astype(jnp.float32), jnp.zeros(grad_input.shape, jnp.float32)
    )
    grad_features = (direct + grad_input).astype(jnp.bfloat16)
    weight_sum_one, weight_sum_two, gain_sum_one, gain_sum_two = lax.psum(
        (weight_grad_one, weight_grad_two, gain_grad_one, gain_grad_two), ("shape", "space")
    )
    total_rows = (
        features.shape[0] * lax.axis_size("shape") * brick_count * peer_count * features.shape[2]
    )
    grad_scale = 1.0 / math.sqrt(total_rows)
    return (
        output.reshape(features.shape),
        grad_features.reshape(features.shape),
        weight_sum_one * grad_scale,
        weight_sum_two * grad_scale,
        gain_sum_one * grad_scale,
        gain_sum_two * grad_scale,
    )


def solution(mesh):
    in_specs = (
        P("shape", "space", None, None),
        P(),
        P(),
        P(),
        P(),
        P("shape", "space"),
        P("shape", "space", None, None),
        P("shape", "space", None),
        P("shape", "space", None, None),
    )
    out_specs = (
        P("shape", "space", None, None),
        P("shape", "space", None, None),
        P(),
        P(),
        P(),
        P(),
    )
    return jax.shard_map(shards, mesh=mesh, in_specs=in_specs, out_specs=out_specs, check_vma=False)
```

profile of v0, /device:TPU:4, one launch (start us, length us, event | category | flops | bytes accessed | tf_op | source)
XLA Modules:
  0.0 569.2 jit_solution(17979509776324319021)
XLA Ops:
  16.4 12.4 %all-to-all-start = ((bf16[64,2,4096]{2,1,0:T(2,128)(2,1)}), bf16[64,2,4096]{2,1,0:T(2,128)(2,1)}, u32[]{:S(2)}, u32[]{:S(2)}) async-start(bf16[64,2,4096]{2,1,0:T(2,128)(2,1)} %reshape.1985), calls=%async_computation | async-start | bytes 2097152 | tf_op jit(solution)/shard_map/all_to_all | solution.py:153
  31.3 2.7 scatter-add.89
  34.3 2.7 scatter-add.90
  37.2 2.7 scatter-add.91
  40.1 2.7 scatter-add.94
  43.3 2.7 scatter-add.96
  54.3 3.3 reduce.80
  60.2 11.2 %all-to-all-start.2 = ((bf16[64,2,4096]{2,1,0:T(2,128)(2,1)}), bf16[64,2,4096]{2,1,0:T(2,128)(2,1)}, u32[]{:S(2)}, u32[]{:S(2)}) async-start(bf16[64,2,4096]{2,1,0:T(2,128)(2,1)} %reshape.1989), calls=%async_computation.2 | async-start | bytes 2097152 | tf_op jit(solution)/shard_map/all_to_all | solution.py:171
  71.4 7.5 %reshape.1986 = bf16[64,1,8192]{2,1,0:T(2,128)(2,1)} reshape(bf16[64,2,4096]{2,1,0:T(2,128)(2,1)} %all-to-all-done) | data formatting | bytes 2097152
  78.9 2.8 convolution_convert_fusion.5
  88.9 8.9 %all-to-all-done.2 = bf16[64,2,4096]{2,1,0:T(2,128)(2,1)} async-done(((bf16[64,2,4096]{2,1,0:T(2,128)(2,1)}), bf16[64,2,4096]{2,1,0:T(2,128)(2,1)}, u32[]{:S(2)}, u32[]{:S(2)}) %all-to-all-start.2) | async-done | bytes 1048608 | tf_op jit(solution)/shard_map/all_to_all | solution.py:171
  97.8 7.5 %reshape.1990 = bf16[64,1,8192]{2,1,0:T(2,128)(2,1)} reshape(bf16[64,2,4096]{2,1,0:T(2,128)(2,1)} %all-to-all-done.2) | data formatting | bytes 2097152
  105.3 2.7 copy.213
  118.6 2.9 scatter-add.111
  137.7 8.3 %all-to-all-start.3 = ((bf16[64,2,4096]{2,1,0:T(2,128)(2,1)}), bf16[64,2,4096]{2,1,0:T(2,128)(2,1)}, u32[]{:S(2)}, u32[]{:S(2)}) async-start(bf16[64,2,4096]{2,1,0:T(2,128)(2,1)} %reshape.1991), calls=%async_computation.3 | async-start | bytes 2097152 | tf_op jit(solution)/shard_map/all_to_all | solution.py:171
  152.0 3.3 reduce.82
  164.6 7.9 %all-to-all-done.3 = bf16[64,2,4096]{2,1,0:T(2,128)(2,1)} async-done(((bf16[64,2,4096]{2,1,0:T(2,128)(2,1)}), bf16[64,2,4096]{2,1,0:T(2,128)(2,1)}, u32[]{:S(2)}, u32[]{:S(2)}) %all-to-all-start.3) | async-done | bytes 1048608 | tf_op jit(solution)/shard_map/all_to_all | solution.py:171
  172.6 8.3 %all-to-all-start.1 = ((bf16[64,2,4096]{2,1,0:T(2,128)(2,1)}), bf16[64,2,4096]{2,1,0:T(2,128)(2,1)}, u32[]{:S(2)}, u32[]{:S(2)}) async-start(bf16[64,2,4096]{2,1,0:T(2,128)(2,1)} %reshape.1987), calls=%async_computation.1 | async-start | bytes 2097152 | tf_op jit(solution)/shard_map/all_to_all | solution.py:153
  183.1 7.5 %reshape.1992 = bf16[64,1,8192]{2,1,0:T(2,128)(2,1)} reshape(bf16[64,2,4096]{2,1,0:T(2,128)(2,1)} %all-to-all-done.3) | data formatting | bytes 2097152
  190.6 2.7 copy.212
  197.5 10.0 %all-to-all-done.1 = bf16[64,2,4096]{2,1,0:T(2,128)(2,1)} async-done(((bf16[64,2,4096]{2,1,0:T(2,128)(2,1)}), bf16[64,2,4096]{2,1,0:T(2,128)(2,1)}, u32[]{:S(2)}, u32[]{:S(2)}) %all-to-all-start.1) | async-done | bytes 1048608 | tf_op jit(solution)/shard_map/all_to_all | solution.py:153
  207.5 6.5 %reshape.1988 = bf16[64,1,8192]{2,1,0:T(2,128)(2,1)S(1)} reshape(bf16[64,2,4096]{2,1,0:T(2,128)(2,1)} %all-to-all-done.1) | data formatting | bytes 2097152
  232.3 76.4 %all-reduce.4 = (f32[128]{0:T(128)S(1)}, f32[128]{0:T(128)S(1)}) all-reduce(f32[128]{0:T(128)S(1)} %get-tuple-element.462, f32[128]{0:T(128)S(1)} %get-tuple-element.464), channel_id=1, replica_groups=mesh['shape'=4,'space'=64] {'shape','space'}, use_global_device_ids=true, to_apply=%region_11.12 | all-reduce | flops 256 | bytes 2048 | tf_op jit(solution)/shard_map/psum | solution.py:242
  310.6 249.3 %all-reduce.8.cloned.1.call-done = (f32[7,128,128]{2,1,0:T(8,128)}, f32[7,128,128]{2,1,0:T(8,128)}) async-done(((f32[7,128,128]{2,1,0:T(8,128)}, f32[7,128,128]{2,1,0:T(8,128)}), (f32[7,128,128]{2,1,0:T(8,128)}, f32[7,128,128]{2,1,0:T(8,128)})) %all-reduce.8.cloned.1.call-update) | async-done | bytes 917520 | tf_op jit(solution)/shard_map/psum | solution.py:242
  (252 shorter events, 100.7 us)
Async XLA Ops:
  9.7 2.7 copy-start.4
  9.8 2.3 copy-start.21
  9.8 2.5 copy-start.6
  9.9 2.5 copy-start.26
  16.4 12.6 %copy-start.30 = (s32[1,2]{1,0:T(1,128)S(1)}, s32[1,2]{1,0:T(1,128)}, u32[]{:S(2)}) copy-start(s32[1,2]{1,0:T(1,128)} %param.90) | copy-start | bytes 28
  16.4 12.6 %copy-start.10 = (bf16[1,2,512,128]{3,2,1,0:T(8,128)(2,1)S(1)}, bf16[1,2,512,128]{3,2,1,0:T(8,128)(2,1)}, u32[]{:S(2)}) copy-start(bf16[1,2,512,128]{3,2,1,0:T(8,128)(2,1)} %param.93) | copy-start | bytes 786436
  16.4 43.8 %all-to-all-start = ((bf16[64,2,4096]{2,1,0:T(2,128)(2,1)}), bf16[64,2,4096]{2,1,0:T(2,128)(2,1)}, u32[]{:S(2)}, u32[]{:S(2)}) async-start(bf16[64,2,4096]{2,1,0:T(2,128)(2,1)} %reshape.1985), calls=%async_computation | async-start | bytes 2097152 | tf_op jit(solution)/shard_map/all_to_all | solution.py:153
  31.1 2.9 copy-start.17
  46.7 5.7 %copy-start.23 = (bf16[2,8,8,1,128]{4,3,2,1,0:T(2,128)(2,1)S(1)}, bf16[2,8,8,1,128]{4,3,2,1,0:T(2,128)(2,1)}, u32[]{:S(2)}) copy-start(bf16[2,8,8,1,128]{4,3,2,1,0:T(2,128)(2,1)} %slice.2143) | copy-start | bytes 98308
  60.2 37.6 %all-to-all-start.2 = ((bf16[64,2,4096]{2,1,0:T(2,128)(2,1)}), bf16[64,2,4096]{2,1,0:T(2,128)(2,1)}, u32[]{:S(2)}, u32[]{:S(2)}) async-start(bf16[64,2,4096]{2,1,0:T(2,128)(2,1)} %reshape.1989), calls=%async_computation.2 | async-start | bytes 2097152 | tf_op jit(solution)/shard_map/all_to_all | solution.py:171
  88.4 24.1 %copy-start.13 = (f32[2,8,8,8]{3,2,1,0:T(8,128)}, f32[2,8,8,8]{3,2,1,0:T(8,128)S(1)}, u32[]{:S(2)}) copy-start(f32[2,8,8,8]{3,2,1,0:T(8,128)S(1)} %div.59) | copy-start | bytes 12292
  88.9 23.7 %copy-start.14 = (f32[2,8,8,8]{3,2,1,0:T(8,128)}, f32[2,8,8,8]{3,2,1,0:T(8,128)S(1)}, u32[]{:S(2)}) copy-start(f32[2,8,8,8]{3,2,1,0:T(8,128)S(1)} %rsqrt.23) | copy-start | bytes 12292
  108.3 3.8 copy-start.28
  137.7 34.8 %all-to-all-start.3 = ((bf16[64,2,4096]{2,1,0:T(2,128)(2,1)}), bf16[64,2,4096]{2,1,0:T(2,128)(2,1)}, u32[]{:S(2)}, u32[]{:S(2)}) async-start(bf16[64,2,4096]{2,1,0:T(2,128)(2,1)} %reshape.1991), calls=%async_computation.3 | async-start | bytes 2097152 | tf_op jit(solution)/shard_map/all_to_all | solution.py:171
  146.0 2.1 copy-start.25
  146.0 2.8 copy-start.24
  158.0 2.0 copy-start.1
  172.6 34.9 %all-to-all-start.1 = ((bf16[64,2,4096]{2,1,0:T(2,128)(2,1)}), bf16[64,2,4096]{2,1,0:T(2,128)(2,1)}, u32[]{:S(2)}, u32[]{:S(2)}) async-start(bf16[64,2,4096]{2,1,0:T(2,128)(2,1)} %reshape.1987), calls=%async_computation.1 | async-start | bytes 2097152 | tf_op jit(solution)/shard_map/all_to_all | solution.py:153
  180.9 379.1 %all-reduce.8.cloned.1.call-start = ((), (), s32[]{:S(2)}) async-start(), calls=%async_computation.4 | async-start | bytes 1835008 | tf_op jit(solution)/shard_map/psum | solution.py:242
  226.6 2.9 copy-start.18
  226.7 3.0 copy-start.9
  230.8 78.5 %copy-start.12 = (bf16[1,2,512,128]{3,2,1,0:T(8,128)(2,1)S(1)}, bf16[1,2,512,128]{3,2,1,0:T(8,128)(2,1)}, u32[]{:S(2)}) copy-start(bf16[1,2,512,128]{3,2,1,0:T(8,128)(2,1)} %param.93) | copy-start | bytes 786436
  230.8 78.5 %copy-start.20 = (f32[2,8,8,8]{3,2,1,0:T(8,128)S(1)}, f32[2,8,8,8]{3,2,1,0:T(8,128)}, u32[]{:S(2)}) copy-start(f32[2,8,8,8]{3,2,1,0:T(8,128)} %copy-done.19) | copy-start | bytes 12292
  230.8 78.5 %copy-start.22 = (f32[2,8,8,8]{3,2,1,0:T(8,128)S(1)}, f32[2,8,8,8]{3,2,1,0:T(8,128)}, u32[]{:S(2)}) copy-start(f32[2,8,8,8]{3,2,1,0:T(8,128)} %negate_multiply_fusion) | copy-start | bytes 12292
  (12 other events, 14.6 us)
Sparse Core Ops, SparseCore 0:
  308.8 251.0 all-reduce.7
where the time goes:
time: 579 us; the launch traced here: 569 us
  waiting for transfers between devices  276 us (48%)
  local copies, waits for them, and re-layouts  101 us (17%)
  blocking collectives  76.4 us (13%)
  starting transfers between devices  40.2 us (7%)
  matrix products  32.7 us (6%)
  other arithmetic  27.2 us (5%)
  between operations  15.6 us (3%)
    psum x1, waiting for transfers between devices, shards(): lax.psum((weight_grad_one, weight_grad_two, gain_grad_one, gain_grad_two)...  249 us
    psum x1, blocking collectives, shards(): lax.psum((weight_grad_one, weight_grad_two, gain_grad_one, gain_grad_two)...  76.4 us
    unnamed x106, local copies, waits for them, and re-layouts  53.6 us
    scatter-add x12, local copies, waits for them, and re-layouts, conv_back(): spread = spread.at[:, 1 + step_i:1 + step_i + edge_len, 1 + step_j:1 + st...  27.4 us
    all_to_all x2, starting transfers between devices, trade_faces(): lax.all_to_all(outgoing.reshape(peer_count, slot_count, -1), 'space', spl...  20.7 us
    all_to_all x2, starting transfers between devices, return_slabs(): lax.all_to_all(outgoing.reshape(peer_count, slot_count, -1), 'space', spl...  19.4 us
    all_to_all x2, waiting for transfers between devices, return_slabs(): lax.all_to_all(outgoing.reshape(peer_count, slot_count, -1), 'space', spl...  16.8 us
    dot_general x14, matrix products, conv_back(): lax.dot_general(shifted(padded, tap_index), grad_rows, (((0,), (0,)), (()...  15.3 us
  transfers between devices with their start and end apart: 5, of which 4 were waited for; matrix products, arithmetic and copies ran while one was open for 15% of the time, Pallas kernels for 0%

commit v1 on v0

--- a/solution.py
+++ b/solution.py
@@ -239,8 +239,9 @@
         alive_rows, cot_cube.astype(jnp.float32), jnp.zeros(grad_input.shape, jnp.float32)
     )
     grad_features = (direct + grad_input).astype(jnp.bfloat16)
-    weight_sum_one, weight_sum_two, gain_sum_one, gain_sum_two = lax.psum(
-        (weight_grad_one, weight_grad_two, gain_grad_one, gain_grad_two), ("shape", "space")
+    weight_sum_one, weight_sum_two, gain_sum_one, gain_sum_two = jax.lax.psum(
+        jax.lax.psum((weight_grad_one, weight_grad_two, gain_grad_one, gain_grad_two), "shape"),
+        "space",
     )
     total_rows = (
         features.shape[0] * lax.axis_size("shape") * brick_count * peer_count * features.shape[2]

time: 579 us -> 617 us (1.066)
  blocking collectives: 76.4 us -> 116 us
    psum x1 -> x2, blocking collectives: 76.4 us -> 116 us  [the longest x1 105 us: shards(): jax.lax.psum(jax.lax.psum((weight_grad_one, weight_grad_two, gain_grad_on...]
    psum x1 -> x2, waiting for transfers between devices: 249 us -> 246 us  [the longest x1 188 us: shards(): jax.lax.psum(jax.lax.psum((weight_grad_one, weight_grad_two, gain_grad_on...]
    unnamed x106 -> x104, local copies, waits for them, and re-layouts: 53.6 us -> 53.9 us
  transfers between devices with their start and end apart: 5 -> 6, of which waited for: 4 -> 5; matrix products, arithmetic and copies ran while one was open for 15% -> 14% of each run, Pallas kernels for 0% -> 0%
where the time goes in v1:
time: 617 us; the launch traced here: 606 us
  waiting for transfers between devices  273 us (44%)
  blocking collectives  116 us (19%)
  local copies, waits for them, and re-layouts  101 us (16%)
  starting transfers between devices  40.2 us (7%)
  matrix products  33.6 us (5%)
  other arithmetic  27.1 us (4%)
  between operations  15.5 us (3%)
    psum x1, waiting for transfers between devices, shards(): jax.lax.psum(jax.lax.psum((weight_grad_one, weight_grad_two, gain_grad_on...  188 us
    psum x1, blocking collectives, shards(): jax.lax.psum(jax.lax.psum((weight_grad_one, weight_grad_two, gain_grad_on...  105 us
    psum x1, waiting for transfers between devices, shards(): jax.lax.psum((weight_grad_one, weight_grad_two, gain_grad_one, gain_grad_...  58.5 us
    unnamed x104, local copies, waits for them, and re-layouts  53.9 us
    scatter-add x12, local copies, waits for them, and re-layouts, conv_back(): spread = spread.at[:, 1 + step_i:1 + step_i + edge_len, 1 + step_j:1 + st...  27.4 us
    all_to_all x2, starting transfers between devices, trade_faces(): lax.all_to_all(outgoing.reshape(peer_count, slot_count, -1), 'space', spl...  20.7 us
    all_to_all x2, starting transfers between devices, return_slabs(): lax.all_to_all(outgoing.reshape(peer_count, slot_count, -1), 'space', spl...  19.5 us
    all_to_all x2, waiting for transfers between devices, return_slabs(): lax.all_to_all(outgoing.reshape(peer_count, slot_count, -1), 'space', spl...  16.9 us
  transfers between devices with their start and end apart: 6, of which 5 were waited for; matrix products, arithmetic and copies ran while one was open for 14% of the time, Pallas kernels for 0%

profile of v1, /device:TPU:4, one launch (start us, length us, event | category | flops | bytes accessed | tf_op | source)
XLA Modules:
  0.0 606.4 jit_solution(16481577145022564467)
XLA Ops:
  16.4 12.4 %all-to-all-start = ((bf16[64,2,4096]{2,1,0:T(2,128)(2,1)}), bf16[64,2,4096]{2,1,0:T(2,128)(2,1)}, u32[]{:S(2)}, u32[]{:S(2)}) async-start(bf16[64,2,4096]{2,1,0:T(2,128)(2,1)} %reshape.1985), calls=%async_computation | async-start | bytes 2097152 | tf_op jit(solution)/shard_map/all_to_all | solution.py:153
  31.3 2.7 scatter-add.89
  37.2 2.7 scatter-add.91
  40.1 2.7 scatter-add.94
  54.2 3.3 reduce.80
  60.2 11.2 %all-to-all-start.2 = ((bf16[64,2,4096]{2,1,0:T(2,128)(2,1)}), bf16[64,2,4096]{2,1,0:T(2,128)(2,1)}, u32[]{:S(2)}, u32[]{:S(2)}) async-start(bf16[64,2,4096]{2,1,0:T(2,128)(2,1)} %reshape.1989), calls=%async_computation.2 | async-start | bytes 2097152 | tf_op jit(solution)/shard_map/all_to_all | solution.py:171
  71.4 7.5 %reshape.1986 = bf16[64,1,8192]{2,1,0:T(2,128)(2,1)} reshape(bf16[64,2,4096]{2,1,0:T(2,128)(2,1)} %all-to-all-done) | data formatting | bytes 2097152
  78.9 2.8 convolution_convert_fusion.5
  88.8 8.9 %all-to-all-done.2 = bf16[64,2,4096]{2,1,0:T(2,128)(2,1)} async-done(((bf16[64,2,4096]{2,1,0:T(2,128)(2,1)}), bf16[64,2,4096]{2,1,0:T(2,128)(2,1)}, u32[]{:S(2)}, u32[]{:S(2)}) %all-to-all-start.2) | async-done | bytes 1048608 | tf_op jit(solution)/shard_map/all_to_all | solution.py:171
  97.7 7.5 %reshape.1990 = bf16[64,1,8192]{2,1,0:T(2,128)(2,1)} reshape(bf16[64,2,4096]{2,1,0:T(2,128)(2,1)} %all-to-all-done.2) | data formatting | bytes 2097152
  105.2 2.7 copy.213
  118.5 2.9 scatter-add.111
  137.7 8.3 %all-to-all-start.3 = ((bf16[64,2,4096]{2,1,0:T(2,128)(2,1)}), bf16[64,2,4096]{2,1,0:T(2,128)(2,1)}, u32[]{:S(2)}, u32[]{:S(2)}) async-start(bf16[64,2,4096]{2,1,0:T(2,128)(2,1)} %reshape.1991), calls=%async_computation.3 | async-start | bytes 2097152 | tf_op jit(solution)/shard_map/all_to_all | solution.py:171
  152.0 3.3 reduce.82
  164.6 7.9 %all-to-all-done.3 = bf16[64,2,4096]{2,1,0:T(2,128)(2,1)} async-done(((bf16[64,2,4096]{2,1,0:T(2,128)(2,1)}), bf16[64,2,4096]{2,1,0:T(2,128)(2,1)}, u32[]{:S(2)}, u32[]{:S(2)}) %all-to-all-start.3) | async-done | bytes 1048608 | tf_op jit(solution)/shard_map/all_to_all | solution.py:171
  172.5 8.3 %all-to-all-start.1 = ((bf16[64,2,4096]{2,1,0:T(2,128)(2,1)}), bf16[64,2,4096]{2,1,0:T(2,128)(2,1)}, u32[]{:S(2)}, u32[]{:S(2)}) async-start(bf16[64,2,4096]{2,1,0:T(2,128)(2,1)} %reshape.1987), calls=%async_computation.1 | async-start | bytes 2097152 | tf_op jit(solution)/shard_map/all_to_all | solution.py:153
  183.0 7.5 %reshape.1992 = bf16[64,1,8192]{2,1,0:T(2,128)(2,1)} reshape(bf16[64,2,4096]{2,1,0:T(2,128)(2,1)} %all-to-all-done.3) | data formatting | bytes 2097152
  190.5 2.7 copy.212
  197.4 10.0 %all-to-all-done.1 = bf16[64,2,4096]{2,1,0:T(2,128)(2,1)} async-done(((bf16[64,2,4096]{2,1,0:T(2,128)(2,1)}), bf16[64,2,4096]{2,1,0:T(2,128)(2,1)}, u32[]{:S(2)}, u32[]{:S(2)}) %all-to-all-start.1) | async-done | bytes 1048608 | tf_op jit(solution)/shard_map/all_to_all | solution.py:153
  207.4 6.5 %reshape.1988 = bf16[64,1,8192]{2,1,0:T(2,128)(2,1)S(1)} reshape(bf16[64,2,4096]{2,1,0:T(2,128)(2,1)} %all-to-all-done.1) | data formatting | bytes 2097152
  229.5 10.7 %all-reduce.6 = (f32[128]{0:T(128)S(1)}, f32[128]{0:T(128)S(1)}) all-reduce(f32[128]{0:T(128)S(1)} %get-tuple-element.462, f32[128]{0:T(128)S(1)} %get-tuple-element.464), channel_id=1, replica_groups=mesh['shape'=4,'space'=64] {'shape'}, use_global_device_ids=true, to_apply=%region_13.14 | all-reduce | flops 256 | bytes 2048 | tf_op jit(solution)/shard_map/psum | solution.py:243
  240.3 104.8 %all-reduce.4 = (f32[128]{0:T(128)S(1)}, f32[128]{0:T(128)S(1)}) all-reduce(f32[128]{0:T(128)S(1)} %get-tuple-element.470, f32[128]{0:T(128)S(1)} %get-tuple-element.471), channel_id=1, replica_groups=mesh['shape'=4,'space'=64] {'space'}, use_global_device_ids=true, to_apply=%region_14.15 | all-reduce | flops 256 | bytes 2048 | tf_op jit(solution)/shard_map/psum | solution.py:242
  349.1 58.5 %all-reduce.13.cloned.1.call-done = (f32[7,128,128]{2,1,0:T(8,128)}, f32[7,128,128]{2,1,0:T(8,128)}) async-done(((f32[7,128,128]{2,1,0:T(8,128)}, f32[7,128,128]{2,1,0:T(8,128)}), (f32[7,128,128]{2,1,0:T(8,128)}, f32[7,128,128]{2,1,0:T(8,128)})) %all-reduce.13.cloned.1.call-update) | async-done | bytes 917520 | tf_op jit(solution)/shard_map/psum | solution.py:243
  409.6 187.6 %all-reduce.11.cloned.1.call-done = (f32[7,128,128]{2,1,0:T(8,128)}, f32[7,128,128]{2,1,0:T(8,128)}) async-done(((f32[7,128,128]{2,1,0:T(8,128)}, f32[7,128,128]{2,1,0:T(8,128)}), (f32[7,128,128]{2,1,0:T(8,128)}, f32[7,128,128]{2,1,0:T(8,128)})) %all-reduce.11.cloned.1.call-update) | async-done | bytes 917520 | tf_op jit(solution)/shard_map/psum | solution.py:242
  (254 shorter events, 107.3 us)
Async XLA Ops:
  9.7 2.7 copy-start.4
  9.8 2.3 copy-start.20
  9.8 2.5 copy-start.6
  9.9 2.5 copy-start.25
  16.4 12.6 %copy-start.29 = (s32[1,2]{1,0:T(1,128)S(1)}, s32[1,2]{1,0:T(1,128)}, u32[]{:S(2)}) copy-start(s32[1,2]{1,0:T(1,128)} %param.90) | copy-start | bytes 28
  16.4 12.6 %copy-start.9 = (bf16[1,2,512,128]{3,2,1,0:T(8,128)(2,1)S(1)}, bf16[1,2,512,128]{3,2,1,0:T(8,128)(2,1)}, u32[]{:S(2)}) copy-start(bf16[1,2,512,128]{3,2,1,0:T(8,128)(2,1)} %param.93) | copy-start | bytes 786436
  16.4 43.8 %all-to-all-start = ((bf16[64,2,4096]{2,1,0:T(2,128)(2,1)}), bf16[64,2,4096]{2,1,0:T(2,128)(2,1)}, u32[]{:S(2)}, u32[]{:S(2)}) async-start(bf16[64,2,4096]{2,1,0:T(2,128)(2,1)} %reshape.1985), calls=%async_computation | async-start | bytes 2097152 | tf_op jit(solution)/shard_map/all_to_all | solution.py:153
  31.1 2.9 copy-start.16
  46.7 5.7 copy-start.22
  60.2 37.6 %all-to-all-start.2 = ((bf16[64,2,4096]{2,1,0:T(2,128)(2,1)}), bf16[64,2,4096]{2,1,0:T(2,128)(2,1)}, u32[]{:S(2)}, u32[]{:S(2)}) async-start(bf16[64,2,4096]{2,1,0:T(2,128)(2,1)} %reshape.1989), calls=%async_computation.2 | async-start | bytes 2097152 | tf_op jit(solution)/shard_map/all_to_all | solution.py:171
  88.3 24.2 %copy-start.12 = (f32[2,8,8,8]{3,2,1,0:T(8,128)}, f32[2,8,8,8]{3,2,1,0:T(8,128)S(1)}, u32[]{:S(2)}) copy-start(f32[2,8,8,8]{3,2,1,0:T(8,128)S(1)} %div.59) | copy-start | bytes 12292
  88.8 23.7 %copy-start.13 = (f32[2,8,8,8]{3,2,1,0:T(8,128)}, f32[2,8,8,8]{3,2,1,0:T(8,128)S(1)}, u32[]{:S(2)}) copy-start(f32[2,8,8,8]{3,2,1,0:T(8,128)S(1)} %rsqrt.23) | copy-start | bytes 12292
  108.3 3.8 copy-start.27
  137.7 34.9 %all-to-all-start.3 = ((bf16[64,2,4096]{2,1,0:T(2,128)(2,1)}), bf16[64,2,4096]{2,1,0:T(2,128)(2,1)}, u32[]{:S(2)}, u32[]{:S(2)}) async-start(bf16[64,2,4096]{2,1,0:T(2,128)(2,1)} %reshape.1991), calls=%async_computation.3 | async-start | bytes 2097152 | tf_op jit(solution)/shard_map/all_to_all | solution.py:171
  146.0 2.1 copy-start.24
  146.0 2.8 copy-start.23
  157.9 2.0 copy-start.1
  172.5 34.9 %all-to-all-start.1 = ((bf16[64,2,4096]{2,1,0:T(2,128)(2,1)}), bf16[64,2,4096]{2,1,0:T(2,128)(2,1)}, u32[]{:S(2)}, u32[]{:S(2)}) async-start(bf16[64,2,4096]{2,1,0:T(2,128)(2,1)} %reshape.1987), calls=%async_computation.1 | async-start | bytes 2097152 | tf_op jit(solution)/shard_map/all_to_all | solution.py:153
  180.8 226.9 %all-reduce.13.cloned.1.call-start = ((), (), s32[]{:S(2)}) async-start(), calls=%async_computation.5 | async-start | bytes 1835008 | tf_op jit(solution)/shard_map/psum | solution.py:243
  226.5 2.8 copy-start.17
  229.3 117.0 %copy-start.8 = (bf16[2,8,8,8,128]{4,3,2,1,0:T(8,128)(2,1)S(1)}, bf16[2,8,8,8,128]{4,3,2,1,0:T(8,128)(2,1)}, u32[]{:S(2)}) copy-start(bf16[2,8,8,8,128]{4,3,2,1,0:T(8,128)(2,1)} %get-tuple-element.480) | copy-start | bytes 786436
  345.1 252.1 %all-reduce.11.cloned.1.call-start = ((), (), s32[]{:S(2)}) async-start(), calls=%async_computation.4 | async-start | bytes 1835008 | tf_op jit(solution)/shard_map/psum | solution.py:242
  347.6 60.6 %copy-start.11 = (bf16[1,2,512,128]{3,2,1,0:T(8,128)(2,1)S(1)}, bf16[1,2,512,128]{3,2,1,0:T(8,128)(2,1)}, u32[]{:S(2)}) copy-start(bf16[1,2,512,128]{3,2,1,0:T(8,128)(2,1)} %param.93) | copy-start | bytes 786436
  347.6 60.6 %copy-start.19 = (f32[2,8,8,8]{3,2,1,0:T(8,128)S(1)}, f32[2,8,8,8]{3,2,1,0:T(8,128)}, u32[]{:S(2)}) copy-start(f32[2,8,8,8]{3,2,1,0:T(8,128)} %copy-done.18) | copy-start | bytes 12292
  (12 other events, 13.6 us)
Sparse Core Ops, SparseCore 0:
  345.2 62.4 all-reduce.12
  411.1 185.9 all-reduce.10
